TPU v7x, 256 devices: a whole 4x4x8 slice. The times are simulated.
256 devices in a mesh: pair: 64 (over y_hi, z, x), row: 4 (over y_lo, core).
Axes of the slice: x: 4, y: 4 (y_hi: 2, y_lo: 2; y = y_hi * 2 + y_lo), z: 8, core: 2. Of those that a mesh axis runs over, the one named last changes fastest.
Arguments:
- states: float32 [8192, 32768], P('row', 'pair'), may hold values from -40 to 40, as said below
Outputs:
- rotated: float32 [8192, 32768], P('row', 'pair')
Inputs may be any that keep to these rules, and one draw needn't show every extreme that they name: Real-valued states of full rank.
All inputs are finite; a program needn't handle non-finite values.
Results may differ from a plain program's by a relative error of at most 0.0001.
Values sent between devices are 32-bit elements; how exact they have to be, the bound alone decides.
A program may use at most 64 MiB of HBM per device.

v0:
```python
import jax
import jax.numpy as jnp
from jax import lax
from jax.sharding import PartitionSpec as P

ROUNDS = 2
NS_STEPS = 2


highest = lax.Precision.HIGHEST


def from_behind(value, axis, steps):
    count = lax.axis_size(axis)
    first, last = (max(0, -steps), min(count, count - steps))
    return lax.ppermute(value, axis, [(source, source + steps) for source in range(first, last)])


def inner(left, right):
    return jnp.dot(left.T, right, precision=highest, preferred_element_type=jnp.float32)


def product(left, right):
    return jnp.dot(left, right, precision=highest, preferred_element_type=jnp.float32)


def rotation(gram, width):
    diag = jnp.diagonal(gram)
    first = diag[:width]
    second = diag[width:]
    cross = gram[:width, width:]
    gap = second[None, :] - first[:, None]
    raw = cross * gap / (gap * gap + first[:, None] * second[None, :] + 1e-06)
    theta = raw / (1.0 + jnp.sqrt(jnp.sum(raw * raw)))
    ident = jnp.eye(width, dtype=jnp.float32)
    upper = jnp.concatenate([ident, theta], axis=1)
    lower = jnp.concatenate([-theta.T, ident], axis=1)
    mat = jnp.concatenate([upper, lower], axis=0)
    for step in range(NS_STEPS):
        mat = 1.5 * mat - 0.5 * product(mat, inner(mat, mat))
    return mat


def summed_gram(pair):
    return lax.psum(inner(pair, pair), "row")


def shards(states):
    width = states.shape[1] // 2
    index = lax.axis_index("pair")
    last = lax.axis_size("pair") - 1
    top = states[:, :width]
    bottom = states[:, width:]
    for step in range(ROUNDS):
        pair = jnp.concatenate([top, bottom], axis=1)
        gram = summed_gram(pair)
        turn = rotation(gram, width)
        pair = product(pair, turn)
        top = pair[:, :width]
        bottom = pair[:, width:]
        if step + 1 < ROUNDS:
            leaving = jnp.where(index == 0, bottom, top)
            arrived = from_behind(leaving, "pair", 1)
            from_right = from_behind(bottom, "pair", -1)
            new_top = jnp.where(index == 0, top, arrived)
            new_bottom = jnp.where(index == last, top, from_right)
            top = new_top
            bottom = new_bottom
    return jnp.concatenate([top, bottom], axis=1)


def solution(mesh):
    in_specs = (P("row", "pair"),)
    out_specs = P("row", "pair")
    return jax.shard_map(shards, mesh=mesh, in_specs=in_specs, out_specs=out_specs, check_vma=False)
```

profile of v0, /device:TPU:1, one launch (start us, length us, event | category | flops | bytes accessed | tf_op | source)
XLA Modules:
  0.0 257.0 jit_solution(18255388054066426423)
XLA Ops:
  6.5 11.1 %fusion.26 = f32[512,512]{1,0:T(8,128)} fusion(f32[2048,512]{1,0:T(8,128)} %param.1), kind=kOutput, calls=%fused_computation.49 | convolution fusion | flops 6442450944 | bytes 5242880 | tf_op jit(solution)/shard_map/dot_general | solution.py:20
  17.7 50.8 %all-reduce.3.cloned.1.call-done = f32[512,512]{1,0:T(8,128)} async-done(((f32[512,512]{1,0:T(8,128)}), f32[512,512]{1,0:T(8,128)}) %all-reduce.3.cloned.1.call-update) | async-done | bytes 1048592 | tf_op jit(solution)/shard_map/psum | solution.py:45
  68.5 9.1 %gather_fusion = f32[512]{0:T(512)S(1)} fusion(f32[512,512]{1,0:T(8,128)} %all-reduce.3.cloned.1.call-done, s32[512]{0:T(512)S(1)} %bitcast.22), kind=kCustom, calls=%fused_computation | custom fusion | bytes 8192 | tf_op jit(solution)/shard_map/jit(diagonal)/cond/branch_0_fun/gather | solution.py:28
  77.8 0.1 copy.10
  77.9 1.0 slice_multiply_fusion
  78.9 0.1 copy.11
  79.0 0.8 multiply_reduce_fusion.1
  80.6 0.1 copy.12
  80.9 1.9 fusion.11
  82.8 1.9 fusion.5
  84.8 1.9 fusion.27
  86.6 2.0 fusion.4
  88.7 7.1 %convolution_bitcast_fusion = f32[2048,512]{0,1:T(8,128)S(1)} fusion(f32[512,512]{0,1:T(8,128)S(1)} %fusion.4, f32[2048,512]{1,0:T(8,128)S(1)} %copy-done), kind=kOutput, calls=%fused_computation.5 | convolution fusion | flops 6442450944 | bytes 9437184 | tf_op jit(solution)/shard_map/dot_general | solution.py:24
  95.7 2.4 slice_select_fusion.2
  98.2 0.8 copy-done.1
  99.0 3.2 %collective-permute-start = (f32[2048,256]{0,1:T(8,128)}, f32[2048,256]{0,1:T(8,128)S(1)}, u32[]{:S(2)}, u32[]{:S(2)}) collective-permute-start(f32[2048,256]{0,1:T(8,128)} %get-tuple-element.11), channel_id=1, source_target_pairs={{0,4},{4,8},{8,12},{12,16},{16,20},{20,24},{24,28},{28,32},{32,36}... | collective-permute-start | bytes 6291464 | tf_op jit(solution)/shard_map/ppermute | solution.py:16
  102.2 1.3 collective-permute-start.1
  103.5 43.6 %collective-permute-done = f32[2048,256]{0,1:T(8,128)S(1)} collective-permute-done((f32[2048,256]{0,1:T(8,128)}, f32[2048,256]{0,1:T(8,128)S(1)}, u32[]{:S(2)}, u32[]{:S(2)}) %collective-permute-start) | collective-permute-done | bytes 2097184 | tf_op jit(solution)/shard_map/ppermute | solution.py:16
  147.1 1.3 copy-done.4
  148.4 2.6 %collective-permute-done.1 = f32[2048,256]{0,1:T(8,128)} collective-permute-done((f32[2048,256]{0,1:T(8,128)}, f32[2048,256]{0,1:T(8,128)}, u32[]{:S(2)}, u32[]{:S(2)}) %collective-permute-start.1) | collective-permute-done | bytes 2097184 | tf_op jit(solution)/shard_map/ppermute | solution.py:16
  151.0 2.8 %slice_select_fusion.1 = (f32[2048,256]{0,1:T(8,128)S(1)}, f32[2048,256]{0,1:T(8,128)S(1)}) fusion(f32[2048,256]{0,1:T(8,128)} %copy-done.4, f32[2048,512]{0,1:T(8,128)} %copy-done.1, pred[]{:T(512)S(6)} %eq.17, f32[2048,256]{0,1:T(8,128)} %collective-permute-done.1, pred[]{:T(512)S(6)} %eq.19), kind=kLoop, calls=%fused_computation.7 | loop fusion | flops 1048576 | bytes 10485762 | tf_op jit(solution)/shard_map/jit(_where)/select_n | solution.py:65
  153.8 1.3 copy-done.2
  155.1 8.0 %fusion.1 = f32[512,512]{0,1:T(8,128)} fusion(f32[2048,256]{0,1:T(8,128)S(1)} %get-tuple-element.10, f32[2048,256]{0,1:T(8,128)S(1)} %get-tuple-element.9), kind=kOutput, calls=%fused_computation.4 | convolution fusion | flops 6443499520 | bytes 5242880 | tf_op jit(solution)/shard_map/dot_general | solution.py:20
  163.1 51.4 %all-reduce.5.cloned.1.call-done = f32[512,512]{0,1:T(8,128)} async-done(((f32[512,512]{0,1:T(8,128)}), f32[512,512]{0,1:T(8,128)}) %all-reduce.5.cloned.1.call-update) | async-done | bytes 1048592 | tf_op jit(solution)/shard_map/psum | solution.py:45
  214.5 8.8 %gather_fusion.1 = f32[512]{0:T(512)S(1)} fusion(f32[512,512]{0,1:T(8,128)} %all-reduce.5.cloned.1.call-done, s32[512]{0:T(512)S(1)} %bitcast.23), kind=kCustom, calls=%fused_computation.1 | custom fusion | bytes 8192 | tf_op jit(solution)/shard_map/jit(diagonal)/cond/branch_0_fun/gather | solution.py:28
  223.3 1.8 multiply_reduce_fusion
  225.7 1.1 negate_bitcast_fusion
  227.0 1.9 fusion.8
  228.9 2.0 fusion.3
  230.8 1.9 fusion.28
  232.7 1.9 fusion.2
  234.6 15.3 %fusion = f32[2048,512]{1,0:T(8,128)} fusion(f32[512,512]{0,1:T(8,128)S(1)} %fusion.2, f32[2048,256]{0,1:T(8,128)S(1)} %copy-done.3, f32[2048,256]{0,1:T(8,128)S(1)} %get-tuple-element.9), kind=kOutput, calls=%fused_computation.3 | convolution fusion | flops 6443499520 | bytes 9437184 | tf_op jit(solution)/shard_map/dot_general | solution.py:24
  (20 shorter events, 0.7 us)
Async XLA Ops:
  6.5 62.0 %all-reduce.3.cloned.1.call-start = ((), (), s32[]{:S(2)}) async-start(), calls=%async_computation | async-start | bytes 2097152 | tf_op jit(solution)/shard_map/psum | solution.py:45
  17.7 196.8 %all-reduce.5.cloned.1.call-start = ((), (), s32[]{:S(2)}) async-start(), calls=%async_computation.1 | async-start | bytes 2097152 | tf_op jit(solution)/shard_map/psum | solution.py:45
  84.8 3.9 %copy-start = (f32[2048,512]{1,0:T(8,128)S(1)}, f32[2048,512]{1,0:T(8,128)}, u32[]{:S(2)}) copy-start(f32[2048,512]{1,0:T(8,128)} %param.1) | copy-start | bytes 12582916
  95.7 3.3 %copy-start.1 = (f32[2048,512]{0,1:T(8,128)}, f32[2048,512]{0,1:T(8,128)S(1)}, u32[]{:S(2)}) copy-start(f32[2048,512]{0,1:T(8,128)S(1)} %convolution_bitcast_fusion) | copy-start | bytes 12582916
  99.0 48.1 %collective-permute-start = (f32[2048,256]{0,1:T(8,128)}, f32[2048,256]{0,1:T(8,128)S(1)}, u32[]{:S(2)}, u32[]{:S(2)}) collective-permute-start(f32[2048,256]{0,1:T(8,128)} %get-tuple-element.11), channel_id=1, source_target_pairs={{0,4},{4,8},{8,12},{12,16},{16,20},{20,24},{24,28},{28,32},{32,36}... | collective-permute-start | bytes 6291464 | tf_op jit(solution)/shard_map/ppermute | solution.py:16
  102.2 48.8 %collective-permute-start.1 = (f32[2048,256]{0,1:T(8,128)}, f32[2048,256]{0,1:T(8,128)}, u32[]{:S(2)}, u32[]{:S(2)}) collective-permute-start(f32[2048,256]{0,1:T(8,128)} %get-tuple-element.12), channel_id=1, source_target_pairs={{4,0},{8,4},{12,8},{16,12},{20,16},{24,20},{28,24},{32,28},{36,32}... | collective-permute-start | bytes 6291464 | tf_op jit(solution)/shard_map/ppermute | solution.py:16
  147.1 1.3 copy-start.4
  153.8 1.3 copy-start.2
  230.8 3.8 %copy-start.3 = (f32[2048,256]{0,1:T(8,128)S(1)}, f32[2048,256]{0,1:T(8,128)}, u32[]{:S(2)}) copy-start(f32[2048,256]{0,1:T(8,128)} %copy-done.2) | copy-start | bytes 6291460
Sparse Core Ops, SparseCore 0:
  17.8 50.7 all-reduce.2
  163.2 51.2 all-reduce.4
where the time goes:
time: 261 us; the launch traced here: 257 us
  waiting for transfers between devices  148 us (57%)
  matrix products  56.7 us (22%)
  local copies, waits for them, and re-layouts  22 us (8%)
  between operations  15.3 us (6%)
  other arithmetic  10.2 us (4%)
  starting transfers between devices  4.54 us (2%)
    psum x2, waiting for transfers between devices, summed_gram(): return lax.psum(inner(pair, pair), 'row')  102 us
    ppermute x2, waiting for transfers between devices, from_behind(): lax.ppermute(value, axis, [(source, source + steps) for source in range(f...  46.2 us
    dot_general x6, matrix products, product(): jnp.dot(left, right, precision=highest, preferred_element_type=jnp.float32)  30.1 us
    dot_general x6, matrix products, inner(): jnp.dot(left.T, right, precision=highest, preferred_element_type=jnp.floa...  26.5 us
    gather x2, local copies, waits for them, and re-layouts, rotation(): diag = jnp.diagonal(gram)  17.9 us
  transfers between devices with their start and end apart: 4, of which 4 were waited for; matrix products, arithmetic and copies ran while one was open for 0% of the time, Pallas kernels for 0%

commit v1 on v0

v1 whole, which is shorter than its diff:
```python
import functools

import jax
import jax.numpy as jnp
from jax import lax
from jax.experimental import pallas as pl
from jax.experimental.pallas import tpu as pltpu
from jax.sharding import PartitionSpec as P

MESH = pl.DeviceIdType.MESH
F32 = jnp.float32
BF16 = jnp.bfloat16
EXTRA = 8
PIECES = 2


def split(value):
    high = value.astype(BF16)
    return high, (value - high.astype(F32)).astype(BF16)


def dot(left, right, dims):
    return lax.dot_general(left, right, (dims, ((), ())), preferred_element_type=F32)


def dot3(left, right, dims=((1,), (0,))):
    lh, ll = left
    rh, rl = right
    return dot(lh, rh, dims) + (dot(lh, rl, dims) + dot(ll, rh, dims))


def inner(left, right):
    return dot3(left, right, ((0,), (0,)))


def column_sums(value):
    rows, width = value.shape
    return jnp.sum((value * value).reshape(rows // EXTRA, EXTRA, width), axis=0)


def angles(cross, first, second):
    width = cross.shape[0]
    first = jnp.broadcast_to(first, (width, width)).T
    second = jnp.broadcast_to(second, (width, width))
    gap = second - first
    raw = cross * gap / (gap * gap + first * second + 1e-06)
    total = jnp.sum(jnp.sum(raw * raw, axis=0, keepdims=True), axis=1, keepdims=True)
    return raw / (1.0 + jnp.sqrt(total))


def polynomial(square, ident):
    halves = split(square)
    second = dot3(halves, halves)
    factor = 0.375 * ident - 0.3125 * square + 0.0625 * second
    return ident - 0.5 * square + dot3(split(second), split(factor))


def write_turn(theta, high_ref, low_ref):
    width = theta.shape[0]
    rows = lax.broadcasted_iota(jnp.int32, (width, width), 0)
    cols = lax.broadcasted_iota(jnp.int32, (width, width), 1)
    ident = jnp.where(rows == cols, 1.0, 0.0).astype(F32)
    plain = split(theta)
    flipped = split(theta.T)
    upper = polynomial(dot3(plain, flipped), ident)
    lower = polynomial(dot3(flipped, plain), ident)
    off = dot3(split(upper), plain)
    one, two = pl.ds(0, width), pl.ds(width, width)
    for at, block in (((one, one), upper), ((one, two), off), ((two, one), -off.T), ((two, two), lower)):
        high, low = split(block)
        high_ref[at] = high
        low_ref[at] = low


def exchange_kernel(
    n_pair, chunk, load,
    x_ref, pair_ref, high_ref, low_ref,
    top, bot, new_top, new_bot, part, got, full, acc, sums, turn_high, turn_low,
    load_sem, send_sem, recv_sem, store_sem, row_send, row_recv,
):
    p = lax.axis_index("pair")
    row = lax.axis_index("row")
    core = lax.rem(row, 2)
    mate = row + 1 - 2 * core
    across = lax.rem(row + 2, 4)
    samples, width = top.shape
    n_chunks = samples // chunk
    first = p == 0
    last = p == n_pair - 1

    loads = []
    for i in range(samples // load):
        at = pl.ds(i * load, load)
        for half, ref in enumerate((top, bot)):
            copy = pltpu.make_async_copy(
                x_ref.at[at, pl.ds(half * width, width)], ref.at[at], load_sem.at[half, i]
            )
            copy.start()
            loads.append(copy)

    barrier = pltpu.get_barrier_semaphore()

    def greet(**where):
        pl.semaphore_signal(barrier, inc=1, device_id=where, device_id_type=MESH)

    greet(row=mate)
    greet(row=across)

    @pl.when(jnp.logical_not(first))
    def _():
        greet(pair=p - 1)

    @pl.when(jnp.logical_not(last))
    def _():
        greet(pair=p + 1)

    def add_gram(tops, bots, fresh):
        cross = inner(split(tops), split(bots))
        one, two = column_sums(tops), column_sums(bots)
        if fresh:
            acc[...] = cross
            sums[0] = one
            sums[1] = two
        else:
            acc[...] += cross
            sums[0] += one
            sums[1] += two

    def row_sum(turn):
        size = width // 2
        step = size // PIECES

        def piece(k):
            return pl.ds(k * step, step + (EXTRA if k == PIECES - 1 else 0))

        def send(src, dst, stage, k, **where):
            return pltpu.make_async_remote_copy(
                src_ref=src, dst_ref=dst,
                send_sem=row_send.at[turn, stage, k], recv_sem=row_recv.at[turn, stage, k],
                device_id=where, device_id_type=MESH,
            )

        one = lambda k: send(part.at[turn, 1 - core, piece(k)], got.at[turn, 0, piece(k)], 0, k, row=mate)
        two = lambda k: send(part.at[turn, core, piece(k)], got.at[turn, 1, piece(k)], 1, k, row=across)
        three = lambda k: send(full.at[turn, core, piece(k)], full.at[turn, core, piece(k)], 2, k, row=mate)

        for h in range(2):
            part[turn, h, pl.ds(0, size)] = acc[pl.ds(h * size, size)]
            part[turn, h, pl.ds(size, EXTRA)] = sums[h]
        for k in range(PIECES):
            one(k).start()
        for k in range(PIECES):
            one(k).wait()
            part[turn, core, piece(k)] += got[turn, 0, piece(k)]
            two(k).start()
        for k in range(PIECES):
            two(k).wait()
            full[turn, core, piece(k)] = part[turn, core, piece(k)] + got[turn, 1, piece(k)]
            three(k).start()
        for k in range(PIECES):
            three(k).wait()
        cross = jnp.concatenate([full[turn, 0, pl.ds(0, size)], full[turn, 1, pl.ds(0, size)]], axis=0)
        diag = [jnp.sum(full[turn, h, pl.ds(size, EXTRA)], axis=0, keepdims=True) for h in range(2)]
        return angles(cross, *diag)

    for i in range(samples // load):
        loads[2 * i].wait()
        loads[2 * i + 1].wait()
        at = pl.ds(i * load, load)
        add_gram(top[at], bot[at], i == 0)

    @pl.when(jnp.logical_or(first, last))
    def _():
        pl.semaphore_wait(barrier, 3)

    @pl.when(jnp.logical_not(jnp.logical_or(first, last)))
    def _():
        pl.semaphore_wait(barrier, 4)

    write_turn(row_sum(0), turn_high, turn_low)

    def rows_of(i):
        return pl.ds(pl.multiple_of(i * chunk, chunk), chunk)

    def to(src, dst, side, i, **where):
        return pltpu.make_async_remote_copy(
            src_ref=src.at[rows_of(i)], dst_ref=dst.at[rows_of(i)],
            send_sem=send_sem.at[side, i], recv_sem=recv_sem.at[side, i],
            device_id=where, device_id_type=MESH,
        )

    def stays(src, dst, side, i):
        return pltpu.make_async_copy(src.at[rows_of(i)], dst.at[rows_of(i)], recv_sem.at[side, i])

    def rotate(i, carry):
        at = rows_of(i)
        value = split(jnp.concatenate([top[at], bot[at]], axis=1))
        out = dot3(value, (turn_high[...], turn_low[...]))
        top[at] = out[:, :width]
        bot[at] = out[:, width:]

        @pl.when(first)
        def _():
            to(bot, new_top, 0, i, pair=p + 1).start()
            stays(top, new_top, 0, i).start()

        @pl.when(jnp.logical_not(jnp.logical_or(first, last)))
        def _():
            to(top, new_top, 0, i, pair=p + 1).start()

        @pl.when(jnp.logical_not(first))
        def _():
            to(bot, new_bot, 1, i, pair=p - 1).start()

        @pl.when(last)
        def _():
            stays(top, new_bot, 1, i).start()

        return carry

    lax.fori_loop(0, n_chunks, rotate, 0)

    acc[...] = jnp.zeros_like(acc)
    sums[...] = jnp.zeros_like(sums)

    def store(ref, half, i):
        return pltpu.make_async_copy(
            ref.at[rows_of(i)], pair_ref.at[rows_of(i), pl.ds(half * width, width)], store_sem.at[half, i]
        )

    def receive(i, carry):
        @pl.when(first)
        def _():
            stays(top, new_top, 0, i).wait()

        @pl.when(jnp.logical_not(first))
        def _():
            to(top, new_top, 0, i, pair=p - 1).wait_recv()

        @pl.when(last)
        def _():
            stays(top, new_bot, 1, i).wait()

        @pl.when(jnp.logical_not(last))
        def _():
            to(bot, new_bot, 1, i, pair=p + 1).wait_recv()

        store(new_top, 0, i).start()
        store(new_bot, 1, i).start()
        at = rows_of(i)
        add_gram(new_top[at], new_bot[at], False)
        return carry

    lax.fori_loop(0, n_chunks, receive, 0)
    write_turn(row_sum(1), high_ref, low_ref)

    def finish(i, carry):
        store(new_top, 0, i).wait()
        store(new_bot, 1, i).wait()

        @pl.when(jnp.logical_not(last))
        def _():
            to(top, new_top, 0, i, pair=p + 1).wait_send()

        @pl.when(jnp.logical_not(first))
        def _():
            to(bot, new_bot, 1, i, pair=p - 1).wait_send()

        return carry

    lax.fori_loop(0, n_chunks, finish, 0)


def rotate_kernel(x_ref, high_ref, low_ref, out_ref):
    out_ref[...] = dot3(split(x_ref[...]), (high_ref[...], low_ref[...]))


def shards(n_pair, states):
    samples, both = states.shape
    width = both // 2
    chunk = 128
    load = 256
    n_chunks = samples // chunk
    pair, high, low = pl.pallas_call(
        functools.partial(exchange_kernel, n_pair, chunk, load),
        out_shape=[
            jax.ShapeDtypeStruct((samples, both), F32),
            jax.ShapeDtypeStruct((both, both), BF16),
            jax.ShapeDtypeStruct((both, both), BF16),
        ],
        in_specs=[pl.BlockSpec(memory_space=pltpu.HBM)],
        out_specs=[
            pl.BlockSpec(memory_space=pl.ANY),
            pl.BlockSpec(memory_space=pltpu.VMEM),
            pl.BlockSpec(memory_space=pltpu.VMEM),
        ],
        scratch_shapes=[pltpu.VMEM((samples, width), F32)] * 4
        + [
            pltpu.VMEM((2, 2, width // 2 + EXTRA, width), F32),
            pltpu.VMEM((2, 2, width // 2 + EXTRA, width), F32),
            pltpu.VMEM((2, 2, width // 2 + EXTRA, width), F32),
            pltpu.VMEM((width, width), F32),
            pltpu.VMEM((2, EXTRA, width), F32),
            pltpu.VMEM((both, both), BF16),
            pltpu.VMEM((both, both), BF16),
            pltpu.SemaphoreType.DMA((2, samples // load)),
            pltpu.SemaphoreType.DMA((2, n_chunks)),
            pltpu.SemaphoreType.DMA((2, n_chunks)),
            pltpu.SemaphoreType.DMA((2, n_chunks)),
            pltpu.SemaphoreType.DMA((2, 3, PIECES)),
            pltpu.SemaphoreType.DMA((2, 3, PIECES)),
        ],
        compiler_params=pltpu.CompilerParams(
            collective_id=0, has_side_effects=True, vmem_limit_bytes=40 * 2**20
        ),
        name="exchange",
    )(states)
    tile = 256
    return pl.pallas_call(
        rotate_kernel,
        grid=(samples // tile,),
        out_shape=jax.ShapeDtypeStruct((samples, both), F32),
        in_specs=[
            pl.BlockSpec((tile, both), lambda i: (i, 0)),
            pl.BlockSpec((both, both), lambda i: (0, 0)),
            pl.BlockSpec((both, both), lambda i: (0, 0)),
        ],
        out_specs=pl.BlockSpec((tile, both), lambda i: (i, 0)),
        compiler_params=pltpu.CompilerParams(vmem_limit_bytes=20 * 2**20),
        name="rotate",
    )(pair, high, low)


def solution(mesh):
    spec = P("row", "pair")
    return jax.shard_map(
        functools.partial(shards, mesh.shape["pair"]),
        mesh=mesh, in_specs=(spec,), out_specs=spec, check_vma=False,
    )
```

time: 261 us -> 86.8 us (0.33)
  the two profiles are of different devices: /device:TPU:1 before, /device:TPU:17 now
where the time goes in v1:
time: 86.8 us; the launch traced here: 86.7 us
  Pallas kernels  84.5 us (97%)
  local copies, waits for them, and re-layouts  2.19 us (3%)
    pallas_call x1, Pallas kernels, shards(): pl.pallas_call(functools.partial(exchange_kernel, n_pair, chunk, load), o...  78.3 us
    pallas_call x1, Pallas kernels, shards(): pl.pallas_call(rotate_kernel, grid=(samples // tile,), out_shape=jax.Shap...  6.13 us
    unnamed x2, local copies, waits for them, and re-layouts  2.19 us

profile of v1, /device:TPU:17, one launch (start us, length us, event | category | flops | bytes accessed | tf_op | source)
XLA Modules:
  0.0 86.7 jit_solution(17999515710236736785)
XLA Ops:
  0.0 0.0 copy-start
  0.0 2.2 %copy-done = f32[2048,512]{1,0:T(8,128)S(1)} copy-done((f32[2048,512]{1,0:T(8,128)S(1)}, f32[2048,512]{1,0:T(8,128)}, u32[]{:S(2)}) %copy-start) | copy-done | bytes 4194328
  2.2 78.3 %exchange.1 = (f32[2048,512]{1,0:T(8,128)S(1)}, bf16[512,512]{1,0:T(8,128)(2,1)S(1)}, bf16[512,512]{1,0:T(8,128)(2,1)S(1)}) custom-call(f32[2048,512]{1,0:T(8,128)S(1)} %copy-done), custom_call_target="tpu_custom_call" | custom-call | tf_op jit(solution)/shard_map/exchange/pallas_call | solution.py:284
  80.5 6.1 %rotate.1 = f32[2048,512]{1,0:T(8,128)} custom-call(f32[2048,512]{1,0:T(8,128)S(1)} %get-tuple-element.8.x_ref, bf16[512,512]{1,0:T(8,128)(2,1)S(1)} %get-tuple-element.9.high_ref, bf16[512,512]{1,0:T(8,128)(2,1)S(1)} %get-tuple-element.10.low_ref), custom_call_target="tpu_custom_call" | custom-call | tf_op jit(solution)/shard_map/rotate/pallas_call | solution.py:319
Async XLA Ops:
  0.0 2.2 %copy-start = (f32[2048,512]{1,0:T(8,128)S(1)}, f32[2048,512]{1,0:T(8,128)}, u32[]{:S(2)}) copy-start(f32[2048,512]{1,0:T(8,128)} %x_ref.1) | copy-start | bytes 12582916

commit v2 on v1

v2 whole, which is shorter than its diff:
```python
import functools

import jax
import jax.numpy as jnp
from jax import lax
from jax.experimental import pallas as pl
from jax.experimental.pallas import tpu as pltpu
from jax.sharding import PartitionSpec as P

MESH = pl.DeviceIdType.MESH
F32 = jnp.float32
BF16 = jnp.bfloat16
EXTRA = 8
PIECES = 2


def split(value):
    high = value.astype(BF16)
    return high, (value - high.astype(F32)).astype(BF16)


def dot(left, right, dims):
    return lax.dot_general(left, right, (dims, ((), ())), preferred_element_type=F32)


def dot3(left, right, dims=((1,), (0,))):
    lh, ll = left
    rh, rl = right
    return dot(lh, rh, dims) + (dot(lh, rl, dims) + dot(ll, rh, dims))


def inner(left, right):
    return dot3(left, right, ((0,), (0,)))


def column_sums(value):
    rows, width = value.shape
    return jnp.sum((value * value).reshape(rows // EXTRA, EXTRA, width), axis=0)


def angles(cross, first, second):
    width = cross.shape[0]
    first = jnp.broadcast_to(first, (width, width)).T
    second = jnp.broadcast_to(second, (width, width))
    gap = second - first
    raw = cross * gap / (gap * gap + first * second + 1e-06)
    total = jnp.sum(jnp.sum(raw * raw, axis=0, keepdims=True), axis=1, keepdims=True)
    return raw / (1.0 + jnp.sqrt(total))


def polynomial(square, ident):
    halves = split(square)
    second = dot3(halves, halves)
    factor = 0.375 * ident - 0.3125 * square + 0.0625 * second
    return ident - 0.5 * square + dot3(split(second), split(factor))


def write_turn(theta, high_ref, low_ref):
    width = theta.shape[0]
    rows = lax.broadcasted_iota(jnp.int32, (width, width), 0)
    cols = lax.broadcasted_iota(jnp.int32, (width, width), 1)
    ident = jnp.where(rows == cols, 1.0, 0.0).astype(F32)
    plain = split(theta)
    flipped = split(theta.T)
    upper = polynomial(dot3(plain, flipped), ident)
    lower = polynomial(dot3(flipped, plain), ident)
    off = dot3(split(upper), plain)
    one, two = pl.ds(0, width), pl.ds(width, width)
    for half, at, block in ((0, one, upper), (1, one, off), (0, two, -off.T), (1, two, lower)):
        high, low = split(block)
        high_ref[half, at] = high
        low_ref[half, at] = low


def exchange_kernel(
    n_pair, chunk, load, early,
    x_ref, pair_ref, high_ref, low_ref,
    x, out, raw, part, got, full, acc, sums, theta_own, thetas, turn_high, turn_low, early_high, early_low, relay,
    load_sem, send_sem, recv_sem, raw_send, raw_recv, theta_send, theta_recv, share_send, share_recv, row_send, row_recv,
    relay_send, relay_recv,
):
    p = lax.axis_index("pair")
    row = lax.axis_index("row")
    core = lax.rem(row, 2)
    mate = row + 1 - 2 * core
    across = lax.rem(row + 2, 4)
    others = (mate, across, 3 - row)
    samples, both = x.shape
    width = both // 2
    main = samples - early
    n_chunks = main // chunk
    first = p == 0
    last = p == n_pair - 1
    not_first = jnp.logical_not(first)
    not_last = jnp.logical_not(last)
    seam = n_pair // 2
    before = p == seam - 1
    after = p == seam
    ends = jnp.logical_or(first, last)
    middle = jnp.logical_or(before, after)
    rightward = jnp.logical_and(not_last, jnp.logical_not(before))
    leftward = jnp.logical_and(not_first, jnp.logical_not(after))
    inside = (jnp.logical_and(not_first, jnp.logical_not(after)), jnp.logical_and(not_last, jnp.logical_not(before)))
    halves = pl.ds(0, width), pl.ds(width, width)

    loads = []
    for i in range(samples // load):
        at = pl.ds(i * load, load)
        loads.append(pltpu.make_async_copy(x_ref.at[at], x.at[at], load_sem.at[i]))
        loads[-1].start()

    barrier = pltpu.get_barrier_semaphore()

    def greet(**where):
        pl.semaphore_signal(barrier, inc=1, device_id=where, device_id_type=MESH)

    for other in others:
        greet(row=other)

    @pl.when(not_first)
    def _():
        greet(pair=p - 1)

    @pl.when(not_last)
    def _():
        greet(pair=p + 1)

    @pl.when(ends)
    def _():
        greet(pair=seam - 1)
        greet(pair=seam)
        pl.semaphore_wait(barrier, 6)

    @pl.when(middle)
    def _():
        greet(pair=0)
        greet(pair=n_pair - 1)
        pl.semaphore_wait(barrier, 7)

    @pl.when(jnp.logical_not(jnp.logical_or(ends, middle)))
    def _():
        pl.semaphore_wait(barrier, 5)

    def send(src, dst, send_sem, recv_sem, **where):
        return pltpu.make_async_remote_copy(
            src_ref=src, dst_ref=dst, send_sem=send_sem, recv_sem=recv_sem, device_id=where, device_id_type=MESH
        )

    def raw_copy(side, **where):
        return send(x_ref.at[pl.ds(main, early)], raw.at[side], raw_send.at[side], raw_recv.at[side], **where)

    @pl.when(rightward)
    def _():
        raw_copy(0, pair=p + 1).start()

    @pl.when(leftward)
    def _():
        raw_copy(1, pair=p - 1).start()

    def add_gram(tops, bots, fresh):
        cross = inner(split(tops), split(bots))
        one, two = column_sums(tops), column_sums(bots)
        if fresh:
            acc[...] = cross
            sums[0] = one
            sums[1] = two
        else:
            acc[...] += cross
            sums[0] += one
            sums[1] += two

    size = width // 2
    step = size // PIECES

    def piece(k):
        return pl.ds(k * step, step + (EXTRA if k == PIECES - 1 else 0))

    def row_copies(turn, k):
        def along(src, dst, stage, other):
            return send(src, dst, row_send.at[turn, stage, k], row_recv.at[turn, stage, k], row=other)

        return (
            along(part.at[turn, 1 - core, piece(k)], got.at[turn, 0, piece(k)], 0, mate),
            along(part.at[turn, core, piece(k)], got.at[turn, 1, piece(k)], 1, across),
            along(full.at[turn, core, piece(k)], full.at[turn, core, piece(k)], 2, mate),
        )

    def row_sum(turn):
        for h in range(2):
            part[turn, h, pl.ds(0, size)] = acc[pl.ds(h * size, size)]
            part[turn, h, pl.ds(size, EXTRA)] = sums[h]
        copies = [row_copies(turn, k) for k in range(PIECES)]
        for one, _, _ in copies:
            one.start()
        for k, (one, two, _) in enumerate(copies):
            one.wait_recv()
            part[turn, core, piece(k)] += got[turn, 0, piece(k)]
            two.start()
        for k, (_, two, three) in enumerate(copies):
            two.wait_recv()
            full[turn, core, piece(k)] = part[turn, core, piece(k)] + got[turn, 1, piece(k)]
            three.start()
        for _, _, three in copies:
            three.wait_recv()
        cross = jnp.concatenate([full[turn, 0, pl.ds(0, size)], full[turn, 1, pl.ds(0, size)]], axis=0)
        diag = [jnp.sum(full[turn, h, pl.ds(size, EXTRA)], axis=0, keepdims=True) for h in range(2)]
        return angles(cross, *diag)

    for i in range(samples // load):
        loads[i].wait()
        at = pl.ds(i * load, load)
        add_gram(x[at, :width], x[at, width:], i == 0)

    theta = row_sum(0)
    theta_own[...] = theta

    def quarter(of):
        return pl.ds(pl.multiple_of(of * (width // 4), width // 4), width // 4)

    def theta_copy(side, q, **where):
        at = quarter((row, across)[q])
        return send(theta_own.at[at], thetas.at[side, at], theta_send.at[side, q], theta_recv.at[side, q], **where)

    @pl.when(rightward)
    def _():
        theta_copy(0, 0, pair=p + 1).start()

    @pl.when(leftward)
    def _():
        theta_copy(1, 0, pair=p - 1).start()

    @pl.when(p == n_pair - 2)
    def _():
        theta_copy(0, 1, pair=p + 1).start()

    @pl.when(p == 1)
    def _():
        theta_copy(1, 1, pair=p - 1).start()

    write_turn(theta, turn_high, turn_low)

    def rows_of(i):
        return pl.ds(pl.multiple_of(i * chunk, chunk), chunk)

    def to(half, side, i, **where):
        return send(
            out.at[half, rows_of(i)], pair_ref.at[rows_of(i), halves[side]],
            send_sem.at[side, i], recv_sem.at[side, i], **where,
        )

    def keep(side, i):
        return pltpu.make_async_copy(out.at[0, rows_of(i)], pair_ref.at[rows_of(i), halves[side]], recv_sem.at[side, i])

    def rotate(i, carry):
        at = rows_of(i)
        value = split(x[at])
        top, bot = (dot3(value, (turn_high[h], turn_low[h])) for h in range(2))
        out[0, at] = top
        out[1, at] = bot

        @pl.when(first)
        def _():
            to(1, 0, i, pair=p + 1).start()
            keep(0, i).start()

        @pl.when(jnp.logical_and(not_first, not_last))
        def _():
            to(0, 0, i, pair=p + 1).start()

        @pl.when(not_first)
        def _():
            to(1, 1, i, pair=p - 1).start()

        @pl.when(last)
        def _():
            keep(1, i).start()

        return carry

    end = pl.ds(main, early)

    def hop(k, src, dst, **where):
        return send(src, dst, relay_send.at[k], relay_recv.at[k], **where)

    def hop_out(**where):
        return hop(0, relay.at[0], relay.at[1], **where)

    def hop_on(side, **where):
        return hop(1, relay.at[1], pair_ref.at[end, halves[side]], **where)

    for half, here, there in ((0, before, n_pair - 1), (1, after, 0)):

        @pl.when(here)
        def _(half=half, there=there):
            relay[0] = dot3(split(x[end]), (turn_high[half], turn_low[half]))
            hop_out(pair=there).start()

    lax.fori_loop(0, n_chunks, rotate, 0)

    for side, here, there in ((0, last, seam), (1, first, seam - 1)):

        @pl.when(here)
        def _(side=side, there=there):
            hop_out(pair=there).wait_recv()
            hop_on(side, pair=there).start()

    def share(side, k, q, of):
        at = quarter(of)
        return send(thetas.at[side, at], thetas.at[side, at], share_send.at[side, k + q], share_recv.at[side, k + q], row=others[k])

    edge = (first, last)
    wide = (last, first)
    narrow = tuple(jnp.logical_and(inside[side], jnp.logical_not(wide[side])) for side in range(2))
    for side in range(2):

        @pl.when(narrow[side])
        def _(side=side):
            theta_copy(side, 0, pair=p).wait_recv()
            for k in range(3):
                share(side, k, 0, row).start()

        @pl.when(wide[side])
        def _(side=side):
            for q in range(2):
                theta_copy(side, q, pair=p).wait_recv()
                share(side, 0, q, (row, across)[q]).start()

        @pl.when(edge[side])
        def _(side=side):
            thetas[side] = theta_own[...]
            raw[side] = x[end]

    for side in range(2):

        @pl.when(narrow[side])
        def _(side=side):
            for k in range(3):
                share(side, k, 0, others[k]).wait_recv()

        @pl.when(wide[side])
        def _(side=side):
            for q in range(2):
                share(side, 0, q, (mate, 3 - row)[q]).wait_recv()

        @pl.when(inside[side])
        def _(side=side):
            raw_copy(side, pair=p).wait_recv()

        @pl.when((after, before)[side])
        def _(side=side):
            hop_on(side, pair=p).wait_recv()

        @pl.when(jnp.logical_not((after, before)[side]))
        def _(side=side):
            write_turn(thetas[side], early_high, early_low)
            half = (p == 1).astype(jnp.int32) if side == 0 else not_last.astype(jnp.int32)
            pair_ref[end, halves[side]] = dot3(split(raw[side]), (early_high[half], early_low[half]))

    add_gram(pair_ref[end, halves[0]], pair_ref[end, halves[1]], True)

    def receive(i, carry):
        keep(0, i).wait()
        keep(1, i).wait()

        at = rows_of(i)
        add_gram(pair_ref[at, halves[0]], pair_ref[at, halves[1]], False)
        return carry

    lax.fori_loop(0, n_chunks, receive, 0)
    write_turn(row_sum(1), high_ref, low_ref)

    def finish(i, carry):
        @pl.when(not_last)
        def _():
            to(0, 0, i, pair=p + 1).wait_send()

        @pl.when(not_first)
        def _():
            to(1, 1, i, pair=p - 1).wait_send()

        return carry

    lax.fori_loop(0, n_chunks, finish, 0)
    for turn in range(2):
        for k in range(PIECES):
            for copy in row_copies(turn, k):
                copy.wait_send()
    for side, goes, twice in ((0, rightward, p == n_pair - 2), (1, leftward, p == 1)):

        @pl.when(goes)
        def _(side=side):
            theta_copy(side, 0, pair=p).wait_send()
            raw_copy(side, pair=p).wait_send()

        @pl.when(twice)
        def _(side=side):
            theta_copy(side, 1, pair=p).wait_send()

        @pl.when(narrow[side])
        def _(side=side):
            for k in range(3):
                share(side, k, 0, row).wait_send()

        @pl.when(wide[side])
        def _(side=side):
            for q in range(2):
                share(side, 0, q, (row, across)[q]).wait_send()
            hop_on(side, pair=p).wait_send()

    @pl.when(middle)
    def _():
        hop_out(pair=p).wait_send()


def rotate_kernel(tiles, x_ref, high_ref, low_ref, out_ref, out, sem):
    copies = []
    at = 0
    for k, rows in enumerate(tiles):
        part = pl.ds(at, rows)
        value = split(x_ref[part])
        out[part] = jnp.concatenate([dot3(value, (high_ref[h], low_ref[h])) for h in range(2)], axis=1)
        copies.append(pltpu.make_async_copy(out.at[part], out_ref.at[part], sem.at[k]))
        copies[-1].start()
        at += rows
    for copy in copies:
        copy.wait()


def shards(n_pair, states):
    samples, both = states.shape
    width = both // 2
    chunk = 128
    load = 256
    early = 256
    main = samples - early
    n_chunks = main // chunk
    turn = (2, both, width)
    pair, high, low = pl.pallas_call(
        functools.partial(exchange_kernel, n_pair, chunk, load, early),
        out_shape=[pltpu.VMEM((samples, both), F32), pltpu.VMEM(turn, BF16), pltpu.VMEM(turn, BF16)],
        in_specs=[pl.BlockSpec(memory_space=pltpu.HBM)],
        out_specs=[pl.BlockSpec(memory_space=pltpu.VMEM)] * 3,
        scratch_shapes=[
            pltpu.VMEM((samples, both), F32),
            pltpu.VMEM((2, main, width), F32),
            pltpu.VMEM((2, early, both), F32),
            pltpu.VMEM((2, 2, width // 2 + EXTRA, width), F32),
            pltpu.VMEM((2, 2, width // 2 + EXTRA, width), F32),
            pltpu.VMEM((2, 2, width // 2 + EXTRA, width), F32),
            pltpu.VMEM((width, width), F32),
            pltpu.VMEM((2, EXTRA, width), F32),
            pltpu.VMEM((width, width), F32),
            pltpu.VMEM((2, width, width), F32),
            pltpu.VMEM(turn, BF16),
            pltpu.VMEM(turn, BF16),
            pltpu.VMEM(turn, BF16),
            pltpu.VMEM(turn, BF16),
            pltpu.VMEM((2, early, width), F32),
            pltpu.SemaphoreType.DMA((samples // load,)),
            pltpu.SemaphoreType.DMA((2, n_chunks)),
            pltpu.SemaphoreType.DMA((2, n_chunks)),
            pltpu.SemaphoreType.DMA((2,)),
            pltpu.SemaphoreType.DMA((2,)),
            pltpu.SemaphoreType.DMA((2, 2)),
            pltpu.SemaphoreType.DMA((2, 2)),
            pltpu.SemaphoreType.DMA((2, 3)),
            pltpu.SemaphoreType.DMA((2, 3)),
            pltpu.SemaphoreType.DMA((2, 3, PIECES)),
            pltpu.SemaphoreType.DMA((2, 3, PIECES)),
            pltpu.SemaphoreType.DMA((2,)),
            pltpu.SemaphoreType.DMA((2,)),
        ],
        compiler_params=pltpu.CompilerParams(
            collective_id=0, has_side_effects=True, vmem_limit_bytes=40 * 2**20
        ),
        name="exchange",
    )(pltpu.with_memory_space_constraint(states, pltpu.HBM))
    tiles = (512, 512, 512, 256, 256)
    return pl.pallas_call(
        functools.partial(rotate_kernel, tiles),
        out_shape=jax.ShapeDtypeStruct((samples, both), F32),
        in_specs=[pl.BlockSpec(memory_space=pltpu.VMEM)] * 3,
        out_specs=pl.BlockSpec(memory_space=pltpu.HBM),
        scratch_shapes=[pltpu.VMEM((samples, both), F32), pltpu.SemaphoreType.DMA((len(tiles),))],
        compiler_params=pltpu.CompilerParams(vmem_limit_bytes=20 * 2**20),
        name="rotate",
    )(pair, high, low)


def solution(mesh):
    spec = P("row", "pair")
    return jax.shard_map(
        functools.partial(shards, mesh.shape["pair"]),
        mesh=mesh, in_specs=(spec,), out_specs=spec, check_vma=False,
    )
```

time: 86.8 us -> 78.9 us (0.909)
  Pallas kernels: 84.5 us -> 78.8 us
  local copies, waits for them, and re-layouts: 2.19 us -> 0 us
    pallas_call x2, Pallas kernels: 84.5 us -> 78.8 us  [the longest x1 74.6 us: shards(): pl.pallas_call(functools.partial(exchange_kernel, n_pair, chunk, load, ea...]
    unnamed x2 -> x0, local copies, waits for them, and re-layouts: 2.19 us -> none
where the time goes in v2:
time: 78.9 us; the launch traced here: 78.8 us
  Pallas kernels  78.8 us (100%)
    pallas_call x1, Pallas kernels, shards(): pl.pallas_call(functools.partial(exchange_kernel, n_pair, chunk, load, ea...  74.6 us
    pallas_call x1, Pallas kernels, shards(): pl.pallas_call(functools.partial(rotate_kernel, tiles), out_shape=jax.Sha...  4.26 us

profile of v2, /device:TPU:17, one launch (start us, length us, event | category | flops | bytes accessed | tf_op | source)
XLA Modules:
  0.0 78.8 jit_solution(4749620087695254524)
XLA Ops:
  0.0 74.6 %exchange.1 = (f32[2048,512]{1,0:T(8,128)S(1)}, bf16[2,512,256]{2,1,0:T(8,128)(2,1)S(1)}, bf16[2,512,256]{2,1,0:T(8,128)(2,1)S(1)}) custom-call(f32[2048,512]{1,0:T(8,128)} %x_ref.1), custom_call_target="tpu_custom_call" | custom-call | tf_op jit(solution)/shard_map/exchange/pallas_call | solution.py:438
  74.6 4.3 %rotate.1 = f32[2048,512]{1,0:T(8,128)} custom-call(f32[2048,512]{1,0:T(8,128)S(1)} %get-tuple-element.8.x_ref, bf16[2,512,256]{2,1,0:T(8,128)(2,1)S(1)} %get-tuple-element.9.high_ref, bf16[2,512,256]{2,1,0:T(8,128)(2,1)S(1)} %get-tuple-element.10.low_ref), custom_call_target="tpu_custom_call" | custom-call | tf_op jit(solution)/shard_map/rotate/pallas_call | solution.py:479

commit v3 on v2

--- a/solution.py
+++ b/solution.py
@@ -12,6 +12,7 @@
 BF16 = jnp.bfloat16
 EXTRA = 8
 PIECES = 2
+MEET = 1
 
 
 def split(value):
@@ -73,11 +74,11 @@
 
 
 def exchange_kernel(
-    n_pair, chunk, load, early,
+    n_pair, chunk, load, early, extra,
     x_ref, pair_ref, high_ref, low_ref,
     x, out, raw, part, got, full, acc, sums, theta_own, thetas, turn_high, turn_low, early_high, early_low, relay,
     load_sem, send_sem, recv_sem, raw_send, raw_recv, theta_send, theta_recv, share_send, share_recv, row_send, row_recv,
-    relay_send, relay_recv,
+    relay_send, relay_recv, far,
 ):
     p = lax.axis_index("pair")
     row = lax.axis_index("row")
@@ -89,6 +90,8 @@
     width = both // 2
     main = samples - early
     n_chunks = main // chunk
+    n_direct = n_chunks - extra // chunk
+    n_hops = (early + extra) // chunk
     first = p == 0
     last = p == n_pair - 1
     not_first = jnp.logical_not(first)
@@ -117,29 +120,45 @@
     for other in others:
         greet(row=other)
 
-    @pl.when(not_first)
-    def _():
-        greet(pair=p - 1)
-
-    @pl.when(not_last)
-    def _():
-        greet(pair=p + 1)
-
-    @pl.when(ends)
-    def _():
-        greet(pair=seam - 1)
-        greet(pair=seam)
-        pl.semaphore_wait(barrier, 6)
-
-    @pl.when(middle)
-    def _():
-        greet(pair=0)
-        greet(pair=n_pair - 1)
-        pl.semaphore_wait(barrier, 7)
-
-    @pl.when(jnp.logical_not(jnp.logical_or(ends, middle)))
-    def _():
-        pl.semaphore_wait(barrier, 5)
+    def meet():
+        @pl.when(jnp.logical_and(not_first, jnp.logical_not(after)))
+        def _():
+            greet(pair=p - 1)
+
+        @pl.when(jnp.logical_and(not_last, jnp.logical_not(before)))
+        def _():
+            greet(pair=p + 1)
+
+        @pl.when(first)
+        def _():
+            greet(pair=seam - 1)
+            greet(pair=seam)
+
+        @pl.when(last)
+        def _():
+            greet(pair=seam - 1)
+
+        @pl.when(after)
+        def _():
+            greet(pair=seam - 1)
+            greet(pair=n_pair - 1)
+
+    meet()
+
+    def met():
+        @pl.when(first)
+        def _():
+            pl.semaphore_wait(barrier, 4)
+
+        @pl.when(before)
+        def _():
+            pl.semaphore_wait(barrier, 7)
+            for there in (0, seam):
+                pl.semaphore_signal(far, inc=1, device_id={"pair": there}, device_id_type=MESH)
+
+        @pl.when(jnp.logical_not(jnp.logical_or(first, before)))
+        def _():
+            pl.semaphore_wait(barrier, 5)
 
     def send(src, dst, send_sem, recv_sem, **where):
         return pltpu.make_async_remote_copy(
@@ -149,13 +168,14 @@
     def raw_copy(side, **where):
         return send(x_ref.at[pl.ds(main, early)], raw.at[side], raw_send.at[side], raw_recv.at[side], **where)
 
-    @pl.when(rightward)
-    def _():
-        raw_copy(0, pair=p + 1).start()
-
-    @pl.when(leftward)
-    def _():
-        raw_copy(1, pair=p - 1).start()
+    def raw_start():
+        @pl.when(rightward)
+        def _():
+            raw_copy(0, pair=p + 1).start()
+
+        @pl.when(leftward)
+        def _():
+            raw_copy(1, pair=p - 1).start()
 
     def add_gram(tops, bots, fresh):
         cross = inner(split(tops), split(bots))
@@ -210,6 +230,9 @@
         loads[i].wait()
         at = pl.ds(i * load, load)
         add_gram(x[at, :width], x[at, width:], i == 0)
+        if i == MEET:
+            met()
+            raw_start()
 
     theta = row_sum(0)
     theta_own[...] = theta
@@ -250,6 +273,12 @@
 
     def keep(side, i):
         return pltpu.make_async_copy(out.at[0, rows_of(i)], pair_ref.at[rows_of(i), halves[side]], recv_sem.at[side, i])
+
+    def goes_right(i):
+        return jnp.logical_and(not_last, jnp.logical_or(jnp.logical_not(before), i < n_direct))
+
+    def goes_left(i):
+        return jnp.logical_and(not_first, jnp.logical_or(jnp.logical_not(after), i < n_direct))
 
     def rotate(i, carry):
         at = rows_of(i)
@@ -263,11 +292,11 @@
             to(1, 0, i, pair=p + 1).start()
             keep(0, i).start()
 
-        @pl.when(jnp.logical_and(not_first, not_last))
+        @pl.when(jnp.logical_and(not_first, goes_right(i)))
         def _():
             to(0, 0, i, pair=p + 1).start()
 
-        @pl.when(not_first)
+        @pl.when(goes_left(i))
         def _():
             to(1, 1, i, pair=p - 1).start()
 
@@ -279,21 +308,29 @@
 
     end = pl.ds(main, early)
 
-    def hop(k, src, dst, **where):
-        return send(src, dst, relay_send.at[k], relay_recv.at[k], **where)
-
-    def hop_out(**where):
-        return hop(0, relay.at[0], relay.at[1], **where)
-
-    def hop_on(side, **where):
-        return hop(1, relay.at[1], pair_ref.at[end, halves[side]], **where)
+    def hop(stage, k, src, dst, **where):
+        return send(src, dst, relay_send.at[stage, k], relay_recv.at[stage, k], **where)
+
+    def hop_out(k, **where):
+        at = pl.ds(k * chunk, chunk)
+        return hop(0, k, relay.at[0, at], relay.at[1, at], **where)
+
+    def hop_on(side, k, **where):
+        to_rows = pl.ds(samples - early - extra + k * chunk, chunk)
+        return hop(1, k, relay.at[1, pl.ds(k * chunk, chunk)], pair_ref.at[to_rows, halves[side]], **where)
+
+    @pl.when(after)
+    def _():
+        pl.semaphore_wait(far, 1)
 
     for half, here, there in ((0, before, n_pair - 1), (1, after, 0)):
 
         @pl.when(here)
         def _(half=half, there=there):
-            relay[0] = dot3(split(x[end]), (turn_high[half], turn_low[half]))
-            hop_out(pair=there).start()
+            for k in range(n_hops):
+                value = split(x[pl.ds(samples - early - extra + k * chunk, chunk)])
+                relay[0, pl.ds(k * chunk, chunk)] = dot3(value, (turn_high[half], turn_low[half]))
+                hop_out(k, pair=there).start()
 
     lax.fori_loop(0, n_chunks, rotate, 0)
 
@@ -301,8 +338,11 @@
 
         @pl.when(here)
         def _(side=side, there=there):
-            hop_out(pair=there).wait_recv()
-            hop_on(side, pair=there).start()
+            if side == 1:
+                pl.semaphore_wait(far, 1)
+            for k in range(n_hops):
+                hop_out(k, pair=there).wait_recv()
+                hop_on(side, k, pair=there).start()
 
     def share(side, k, q, of):
         at = quarter(of)
@@ -346,21 +386,35 @@
         def _(side=side):
             raw_copy(side, pair=p).wait_recv()
 
-        @pl.when((after, before)[side])
-        def _(side=side):
-            hop_on(side, pair=p).wait_recv()
-
         @pl.when(jnp.logical_not((after, before)[side]))
         def _(side=side):
             write_turn(thetas[side], early_high, early_low)
             half = (p == 1).astype(jnp.int32) if side == 0 else not_last.astype(jnp.int32)
             pair_ref[end, halves[side]] = dot3(split(raw[side]), (early_high[half], early_low[half]))
 
-    add_gram(pair_ref[end, halves[0]], pair_ref[end, halves[1]], True)
+    acc[...] = jnp.zeros_like(acc)
+    sums[...] = jnp.zeros_like(sums)
 
     def receive(i, carry):
-        keep(0, i).wait()
-        keep(1, i).wait()
+        @pl.when(jnp.logical_or(jnp.logical_not(after), i < n_direct))
+        def _():
+            keep(0, i).wait()
+
+        @pl.when(jnp.logical_or(jnp.logical_not(before), i < n_direct))
+        def _():
+            keep(1, i).wait()
+
+        @pl.when(i == n_direct)
+        def _():
+            for side in range(2):
+
+                @pl.when((after, before)[side])
+                def _(side=side):
+                    for k in range(n_hops):
+                        hop_on(side, k, pair=p).wait_recv()
+
+            add_gram(pair_ref[end, halves[0]], pair_ref[end, halves[1]], False)
+
 
         at = rows_of(i)
         add_gram(pair_ref[at, halves[0]], pair_ref[at, halves[1]], False)
@@ -370,11 +424,11 @@
     write_turn(row_sum(1), high_ref, low_ref)
 
     def finish(i, carry):
-        @pl.when(not_last)
+        @pl.when(goes_right(i))
         def _():
             to(0, 0, i, pair=p + 1).wait_send()
 
-        @pl.when(not_first)
+        @pl.when(goes_left(i))
         def _():
             to(1, 1, i, pair=p - 1).wait_send()
 
@@ -405,11 +459,13 @@
         def _(side=side):
             for q in range(2):
                 share(side, 0, q, (row, across)[q]).wait_send()
-            hop_on(side, pair=p).wait_send()
+            for k in range(n_hops):
+                hop_on(side, k, pair=p).wait_send()
 
     @pl.when(middle)
     def _():
-        hop_out(pair=p).wait_send()
+        for k in range(n_hops):
+            hop_out(k, pair=p).wait_send()
 
 
 def rotate_kernel(tiles, x_ref, high_ref, low_ref, out_ref, out, sem):
@@ -432,11 +488,12 @@
     chunk = 128
     load = 256
     early = 256
+    extra = 256
     main = samples - early
     n_chunks = main // chunk
     turn = (2, both, width)
     pair, high, low = pl.pallas_call(
-        functools.partial(exchange_kernel, n_pair, chunk, load, early),
+        functools.partial(exchange_kernel, n_pair, chunk, load, early, extra),
         out_shape=[pltpu.VMEM((samples, both), F32), pltpu.VMEM(turn, BF16), pltpu.VMEM(turn, BF16)],
         in_specs=[pl.BlockSpec(memory_space=pltpu.HBM)],
         out_specs=[pl.BlockSpec(memory_space=pltpu.VMEM)] * 3,
@@ -455,7 +512,7 @@
             pltpu.VMEM(turn, BF16),
             pltpu.VMEM(turn, BF16),
             pltpu.VMEM(turn, BF16),
-            pltpu.VMEM((2, early, width), F32),
+            pltpu.VMEM((2, early + extra, width), F32),
             pltpu.SemaphoreType.DMA((samples // load,)),
             pltpu.SemaphoreType.DMA((2, n_chunks)),
             pltpu.SemaphoreType.DMA((2, n_chunks)),
@@ -467,8 +524,9 @@
             pltpu.SemaphoreType.DMA((2, 3)),
             pltpu.SemaphoreType.DMA((2, 3, PIECES)),
             pltpu.SemaphoreType.DMA((2, 3, PIECES)),
-            pltpu.SemaphoreType.DMA((2,)),
-            pltpu.SemaphoreType.DMA((2,)),
+            pltpu.SemaphoreType.DMA((2, (early + extra) // chunk)),
+            pltpu.SemaphoreType.DMA((2, (early + extra) // chunk)),
+            pltpu.SemaphoreType.REGULAR,
         ],
         compiler_params=pltpu.CompilerParams(
             collective_id=0, has_side_effects=True, vmem_limit_bytes=40 * 2**20

time: 78.9 us -> 74.9 us (0.949)
  Pallas kernels: 78.8 us -> 74.6 us
    pallas_call x1, Pallas kernels: 74.6 us -> 70.4 us  [shards(): pl.pallas_call(functools.partial(exchange_kernel, n_pair, chunk, load, ea...]
where the time goes in v3:
time: 74.9 us; the launch traced here: 74.8 us
  Pallas kernels  74.6 us (100%)
    pallas_call x1, Pallas kernels, shards(): pl.pallas_call(functools.partial(exchange_kernel, n_pair, chunk, load, ea...  70.4 us
    pallas_call x1, Pallas kernels, shards(): pl.pallas_call(functools.partial(rotate_kernel, tiles), out_shape=jax.Sha...  4.26 us

profile of v3, /device:TPU:17, one launch (start us, length us, event | category | flops | bytes accessed | tf_op | source)
XLA Modules:
  0.0 74.8 jit_solution(9562834395537656713)
XLA Ops:
  0.0 70.4 %exchange.1 = (f32[2048,512]{1,0:T(8,128)S(1)}, bf16[2,512,256]{2,1,0:T(8,128)(2,1)S(1)}, bf16[2,512,256]{2,1,0:T(8,128)(2,1)S(1)}) custom-call(f32[2048,512]{1,0:T(8,128)} %x_ref.1), custom_call_target="tpu_custom_call" | custom-call | tf_op jit(solution)/shard_map/exchange/pallas_call | solution.py:495
  70.4 4.3 %rotate.1 = f32[2048,512]{1,0:T(8,128)} custom-call(f32[2048,512]{1,0:T(8,128)S(1)} %get-tuple-element.8.x_ref, bf16[2,512,256]{2,1,0:T(8,128)(2,1)S(1)} %get-tuple-element.9.high_ref, bf16[2,512,256]{2,1,0:T(8,128)(2,1)S(1)} %get-tuple-element.10.low_ref), custom_call_target="tpu_custom_call" | custom-call | tf_op jit(solution)/shard_map/rotate/pallas_call | solution.py:537

commit v4 on v3

--- a/solution.py
+++ b/solution.py
@@ -11,8 +11,7 @@
 F32 = jnp.float32
 BF16 = jnp.bfloat16
 EXTRA = 8
-PIECES = 2
-MEET = 1
+PIECES = 1
 
 
 def split(value):
@@ -46,7 +45,7 @@
     gap = second - first
     raw = cross * gap / (gap * gap + first * second + 1e-06)
     total = jnp.sum(jnp.sum(raw * raw, axis=0, keepdims=True), axis=1, keepdims=True)
-    return raw / (1.0 + jnp.sqrt(total))
+    return raw, 1.0 / (1.0 + jnp.sqrt(total))
 
 
 def polynomial(square, ident):
@@ -56,16 +55,16 @@
     return ident - 0.5 * square + dot3(split(second), split(factor))
 
 
-def write_turn(theta, high_ref, low_ref):
+def write_turn(theta, scale, high_ref, low_ref):
     width = theta.shape[0]
     rows = lax.broadcasted_iota(jnp.int32, (width, width), 0)
     cols = lax.broadcasted_iota(jnp.int32, (width, width), 1)
     ident = jnp.where(rows == cols, 1.0, 0.0).astype(F32)
     plain = split(theta)
     flipped = split(theta.T)
-    upper = polynomial(dot3(plain, flipped), ident)
-    lower = polynomial(dot3(flipped, plain), ident)
-    off = dot3(split(upper), plain)
+    upper = polynomial(dot3(plain, flipped) * (scale * scale), ident)
+    lower = polynomial(dot3(flipped, plain) * (scale * scale), ident)
+    off = dot3(split(upper), plain) * scale
     one, two = pl.ds(0, width), pl.ds(width, width)
     for half, at, block in ((0, one, upper), (1, one, off), (0, two, -off.T), (1, two, lower)):
         high, low = split(block)
@@ -76,7 +75,7 @@
 def exchange_kernel(
     n_pair, chunk, load, early, extra,
     x_ref, pair_ref, high_ref, low_ref,
-    x, out, raw, part, got, full, acc, sums, theta_own, thetas, turn_high, turn_low, early_high, early_low, relay,
+    x, out, raw, part, got, full, theta_own, thetas, turn_high, turn_low, early_high, early_low, relay,
     load_sem, send_sem, recv_sem, raw_send, raw_recv, theta_send, theta_recv, share_send, share_recv, row_send, row_recv,
     relay_send, relay_recv, far,
 ):
@@ -177,18 +176,6 @@
         def _():
             raw_copy(1, pair=p - 1).start()
 
-    def add_gram(tops, bots, fresh):
-        cross = inner(split(tops), split(bots))
-        one, two = column_sums(tops), column_sums(bots)
-        if fresh:
-            acc[...] = cross
-            sums[0] = one
-            sums[1] = two
-        else:
-            acc[...] += cross
-            sums[0] += one
-            sums[1] += two
-
     size = width // 2
     step = size // PIECES
 
@@ -205,13 +192,33 @@
             along(full.at[turn, core, piece(k)], full.at[turn, core, piece(k)], 2, mate),
         )
 
-    def row_sum(turn):
+    def add_half(turn, ref, at, h, fresh=False):
+        left = ref[at, pl.ds(pl.multiple_of(h * size, size), size)]
+        value = inner(split(left), split(ref[at, halves[1]]))
+        if fresh:
+            part[turn, h, pl.ds(0, size)] = value
+        else:
+            part[turn, h, pl.ds(0, size)] += value
+
+    def add_sums(turn, ref, at, fresh=False):
         for h in range(2):
-            part[turn, h, pl.ds(0, size)] = acc[pl.ds(h * size, size)]
-            part[turn, h, pl.ds(size, EXTRA)] = sums[h]
+            value = column_sums(ref[at, halves[h]])
+            if fresh:
+                part[turn, h, pl.ds(size, EXTRA)] = value
+            else:
+                part[turn, h, pl.ds(size, EXTRA)] += value
+
+    def add_gram(turn, ref, at):
+        value = inner(split(ref[at, halves[0]]), split(ref[at, halves[1]]))
+        for h in range(2):
+            part[turn, h, pl.ds(0, size)] += value[h * size : (h + 1) * size]
+        add_sums(turn, ref, at)
+
+    def row_sum(turn, finish_own):
         copies = [row_copies(turn, k) for k in range(PIECES)]
         for one, _, _ in copies:
             one.start()
+        finish_own()
         for k, (one, two, _) in enumerate(copies):
             one.wait_recv()
             part[turn, core, piece(k)] += got[turn, 0, piece(k)]
@@ -226,16 +233,20 @@
         diag = [jnp.sum(full[turn, h, pl.ds(size, EXTRA)], axis=0, keepdims=True) for h in range(2)]
         return angles(cross, *diag)
 
+    met()
+    raw_start()
     for i in range(samples // load):
         loads[i].wait()
         at = pl.ds(i * load, load)
-        add_gram(x[at, :width], x[at, width:], i == 0)
-        if i == MEET:
-            met()
-            raw_start()
-
-    theta = row_sum(0)
-    theta_own[...] = theta
+        add_sums(0, x, at, i == 0)
+        add_half(0, x, at, 1 - core, i == 0)
+
+    def finish_own():
+        for i in range(2):
+            add_half(0, x, pl.ds(i * (samples // 2), samples // 2), core, i == 0)
+
+    raw_angles, scale = row_sum(0, finish_own)
+    theta_own[...] = raw_angles * scale
 
     def quarter(of):
         return pl.ds(pl.multiple_of(of * (width // 4), width // 4), width // 4)
@@ -260,7 +271,7 @@
     def _():
         theta_copy(1, 1, pair=p - 1).start()
 
-    write_turn(theta, turn_high, turn_low)
+    write_turn(raw_angles, scale, turn_high, turn_low)
 
     def rows_of(i):
         return pl.ds(pl.multiple_of(i * chunk, chunk), chunk)
@@ -388,14 +399,13 @@
 
         @pl.when(jnp.logical_not((after, before)[side]))
         def _(side=side):
-            write_turn(thetas[side], early_high, early_low)
+            write_turn(thetas[side], 1.0, early_high, early_low)
             half = (p == 1).astype(jnp.int32) if side == 0 else not_last.astype(jnp.int32)
             pair_ref[end, halves[side]] = dot3(split(raw[side]), (early_high[half], early_low[half]))
 
-    acc[...] = jnp.zeros_like(acc)
-    sums[...] = jnp.zeros_like(sums)
-
-    def receive(i, carry):
+    part[1] = jnp.zeros_like(part[1])
+
+    def arrive(i):
         @pl.when(jnp.logical_or(jnp.logical_not(after), i < n_direct))
         def _():
             keep(0, i).wait()
@@ -413,15 +423,20 @@
                     for k in range(n_hops):
                         hop_on(side, k, pair=p).wait_recv()
 
-            add_gram(pair_ref[end, halves[0]], pair_ref[end, halves[1]], False)
-
-
-        at = rows_of(i)
-        add_gram(pair_ref[at, halves[0]], pair_ref[at, halves[1]], False)
+            add_gram(1, pair_ref, end)
+
+
+    def receive(i, carry):
+        arrive(i)
+        add_gram(1, pair_ref, rows_of(i))
         return carry
 
-    lax.fori_loop(0, n_chunks, receive, 0)
-    write_turn(row_sum(1), high_ref, low_ref)
+    lax.fori_loop(0, n_chunks - 1, receive, 0)
+    arrive(n_chunks - 1)
+    tail = pl.ds((n_chunks - 1) * chunk, chunk)
+    add_sums(1, pair_ref, tail)
+    add_half(1, pair_ref, tail, 1 - core)
+    write_turn(*row_sum(1, lambda: add_half(1, pair_ref, tail, core)), high_ref, low_ref)
 
     def finish(i, carry):
         @pl.when(goes_right(i))
@@ -486,9 +501,9 @@
     samples, both = states.shape
     width = both // 2
     chunk = 128
-    load = 256
+    load = 512
     early = 256
-    extra = 256
+    extra = 512
     main = samples - early
     n_chunks = main // chunk
     turn = (2, both, width)
@@ -504,8 +519,6 @@
             pltpu.VMEM((2, 2, width // 2 + EXTRA, width), F32),
             pltpu.VMEM((2, 2, width // 2 + EXTRA, width), F32),
             pltpu.VMEM((2, 2, width // 2 + EXTRA, width), F32),
-            pltpu.VMEM((width, width), F32),
-            pltpu.VMEM((2, EXTRA, width), F32),
             pltpu.VMEM((width, width), F32),
             pltpu.VMEM((2, width, width), F32),
             pltpu.VMEM(turn, BF16),

time: 74.9 us -> 73.9 us (0.987)
  the two profiles are of different devices: /device:TPU:17 before, /device:TPU:1 now
where the time goes in v4:
time: 73.9 us; the launch traced here: 73.6 us
  Pallas kernels  73.5 us (99%)
    pallas_call x1, Pallas kernels, shards(): pl.pallas_call(functools.partial(exchange_kernel, n_pair, chunk, load, ea...  69.2 us
    pallas_call x1, Pallas kernels, shards(): pl.pallas_call(functools.partial(rotate_kernel, tiles), out_shape=jax.Sha...  4.26 us

profile of v4, /device:TPU:1, one launch (start us, length us, event | category | flops | bytes accessed | tf_op | source)
XLA Modules:
  0.0 73.6 jit_solution(9777265659966506260)
XLA Ops:
  0.0 69.2 %exchange.1 = (f32[2048,512]{1,0:T(8,128)S(1)}, bf16[2,512,256]{2,1,0:T(8,128)(2,1)S(1)}, bf16[2,512,256]{2,1,0:T(8,128)(2,1)S(1)}) custom-call(f32[2048,512]{1,0:T(8,128)} %x_ref.1), custom_call_target="tpu_custom_call" | custom-call | tf_op jit(solution)/shard_map/exchange/pallas_call | solution.py:510
  69.2 4.3 %rotate.1 = f32[2048,512]{1,0:T(8,128)} custom-call(f32[2048,512]{1,0:T(8,128)S(1)} %get-tuple-element.8.x_ref, bf16[2,512,256]{2,1,0:T(8,128)(2,1)S(1)} %get-tuple-element.9.high_ref, bf16[2,512,256]{2,1,0:T(8,128)(2,1)S(1)} %get-tuple-element.10.low_ref), custom_call_target="tpu_custom_call" | custom-call | tf_op jit(solution)/shard_map/rotate/pallas_call | solution.py:550

commit v5 on v4

--- a/solution.py
+++ b/solution.py
@@ -214,7 +214,7 @@
             part[turn, h, pl.ds(0, size)] += value[h * size : (h + 1) * size]
         add_sums(turn, ref, at)
 
-    def row_sum(turn, finish_own):
+    def row_sum(turn, finish_own, meanwhile=lambda: None):
         copies = [row_copies(turn, k) for k in range(PIECES)]
         for one, _, _ in copies:
             one.start()
@@ -223,6 +223,7 @@
             one.wait_recv()
             part[turn, core, piece(k)] += got[turn, 0, piece(k)]
             two.start()
+        meanwhile()
         for k, (_, two, three) in enumerate(copies):
             two.wait_recv()
             full[turn, core, piece(k)] = part[turn, core, piece(k)] + got[turn, 1, piece(k)]
@@ -436,51 +437,54 @@
     tail = pl.ds((n_chunks - 1) * chunk, chunk)
     add_sums(1, pair_ref, tail)
     add_half(1, pair_ref, tail, 1 - core)
-    write_turn(*row_sum(1, lambda: add_half(1, pair_ref, tail, core)), high_ref, low_ref)
-
-    def finish(i, carry):
-        @pl.when(goes_right(i))
-        def _():
-            to(0, 0, i, pair=p + 1).wait_send()
-
-        @pl.when(goes_left(i))
-        def _():
-            to(1, 1, i, pair=p - 1).wait_send()
-
-        return carry
-
-    lax.fori_loop(0, n_chunks, finish, 0)
-    for turn in range(2):
+    def drain():
+        def finish(i, carry):
+            @pl.when(goes_right(i))
+            def _():
+                to(0, 0, i, pair=p + 1).wait_send()
+
+            @pl.when(goes_left(i))
+            def _():
+                to(1, 1, i, pair=p - 1).wait_send()
+
+            return carry
+
+        lax.fori_loop(0, n_chunks, finish, 0)
         for k in range(PIECES):
-            for copy in row_copies(turn, k):
+            for copy in row_copies(0, k):
                 copy.wait_send()
-    for side, goes, twice in ((0, rightward, p == n_pair - 2), (1, leftward, p == 1)):
-
-        @pl.when(goes)
-        def _(side=side):
-            theta_copy(side, 0, pair=p).wait_send()
-            raw_copy(side, pair=p).wait_send()
-
-        @pl.when(twice)
-        def _(side=side):
-            theta_copy(side, 1, pair=p).wait_send()
-
-        @pl.when(narrow[side])
-        def _(side=side):
-            for k in range(3):
-                share(side, k, 0, row).wait_send()
-
-        @pl.when(wide[side])
-        def _(side=side):
-            for q in range(2):
-                share(side, 0, q, (row, across)[q]).wait_send()
+        for side, goes, twice in ((0, rightward, p == n_pair - 2), (1, leftward, p == 1)):
+
+            @pl.when(goes)
+            def _(side=side):
+                theta_copy(side, 0, pair=p).wait_send()
+                raw_copy(side, pair=p).wait_send()
+
+            @pl.when(twice)
+            def _(side=side):
+                theta_copy(side, 1, pair=p).wait_send()
+
+            @pl.when(narrow[side])
+            def _(side=side):
+                for k in range(3):
+                    share(side, k, 0, row).wait_send()
+
+            @pl.when(wide[side])
+            def _(side=side):
+                for q in range(2):
+                    share(side, 0, q, (row, across)[q]).wait_send()
+                for k in range(n_hops):
+                    hop_on(side, k, pair=p).wait_send()
+
+        @pl.when(middle)
+        def _():
             for k in range(n_hops):
-                hop_on(side, k, pair=p).wait_send()
-
-    @pl.when(middle)
-    def _():
-        for k in range(n_hops):
-            hop_out(k, pair=p).wait_send()
+                hop_out(k, pair=p).wait_send()
+
+    write_turn(*row_sum(1, lambda: add_half(1, pair_ref, tail, core), drain), high_ref, low_ref)
+    for k in range(PIECES):
+        for copy in row_copies(1, k):
+            copy.wait_send()
 
 
 def rotate_kernel(tiles, x_ref, high_ref, low_ref, out_ref, out, sem):

time: 73.9 us -> 73.6 us (level)
  no operation moved by 1% of the time
where the time goes in v5:
time: 73.6 us; the launch traced here: 73.4 us
  Pallas kernels  73.2 us (99%)
    pallas_call x1, Pallas kernels, shards(): pl.pallas_call(functools.partial(exchange_kernel, n_pair, chunk, load, ea...  69 us
    pallas_call x1, Pallas kernels, shards(): pl.pallas_call(functools.partial(rotate_kernel, tiles), out_shape=jax.Sha...  4.26 us

profile of v5, /device:TPU:1, one launch (start us, length us, event | category | flops | bytes accessed | tf_op | source)
XLA Modules:
  0.0 73.4 jit_solution(14042522385902110103)
XLA Ops:
  0.0 69.0 %exchange.1 = (f32[2048,512]{1,0:T(8,128)S(1)}, bf16[2,512,256]{2,1,0:T(8,128)(2,1)S(1)}, bf16[2,512,256]{2,1,0:T(8,128)(2,1)S(1)}) custom-call(f32[2048,512]{1,0:T(8,128)} %x_ref.1), custom_call_target="tpu_custom_call" | custom-call | tf_op jit(solution)/shard_map/exchange/pallas_call | solution.py:514
  69.0 4.3 %rotate.1 = f32[2048,512]{1,0:T(8,128)} custom-call(f32[2048,512]{1,0:T(8,128)S(1)} %get-tuple-element.8.x_ref, bf16[2,512,256]{2,1,0:T(8,128)(2,1)S(1)} %get-tuple-element.9.high_ref, bf16[2,512,256]{2,1,0:T(8,128)(2,1)S(1)} %get-tuple-element.10.low_ref), custom_call_target="tpu_custom_call" | custom-call | tf_op jit(solution)/shard_map/rotate/pallas_call | solution.py:554

commit v6 on v5

--- a/solution.py
+++ b/solution.py
@@ -504,7 +504,7 @@
 def shards(n_pair, states):
     samples, both = states.shape
     width = both // 2
-    chunk = 128
+    chunk = 256
     load = 512
     early = 256
     extra = 512

time: 73.6 us -> 73.1 us (level)
  no operation moved by 1% of the time
where the time goes in v6:
time: 73.1 us; the launch traced here: 73 us
  Pallas kernels  72.9 us (100%)
    pallas_call x1, Pallas kernels, shards(): pl.pallas_call(functools.partial(exchange_kernel, n_pair, chunk, load, ea...  68.6 us
    pallas_call x1, Pallas kernels, shards(): pl.pallas_call(functools.partial(rotate_kernel, tiles), out_shape=jax.Sha...  4.26 us

profile of v6, /device:TPU:1, one launch (start us, length us, event | category | flops | bytes accessed | tf_op | source)
XLA Modules:
  0.0 73.0 jit_solution(10319563737533405008)
XLA Ops:
  0.0 68.6 %exchange.1 = (f32[2048,512]{1,0:T(8,128)S(1)}, bf16[2,512,256]{2,1,0:T(8,128)(2,1)S(1)}, bf16[2,512,256]{2,1,0:T(8,128)(2,1)S(1)}) custom-call(f32[2048,512]{1,0:T(8,128)} %x_ref.1), custom_call_target="tpu_custom_call" | custom-call | tf_op jit(solution)/shard_map/exchange/pallas_call | solution.py:514
  68.6 4.3 %rotate.1 = f32[2048,512]{1,0:T(8,128)} custom-call(f32[2048,512]{1,0:T(8,128)S(1)} %get-tuple-element.8.x_ref, bf16[2,512,256]{2,1,0:T(8,128)(2,1)S(1)} %get-tuple-element.9.high_ref, bf16[2,512,256]{2,1,0:T(8,128)(2,1)S(1)} %get-tuple-element.10.low_ref), custom_call_target="tpu_custom_call" | custom-call | tf_op jit(solution)/shard_map/rotate/pallas_call | solution.py:554
